TPU v7x, 256 devices: a whole 4x4x8 slice. The times are simulated.
256 devices in a mesh: dp: 16 (over x_hi, z), seq: 16 (over y, x_lo, core).
Axes of the slice: x: 4 (x_hi: 2, x_lo: 2; x = x_hi * 2 + x_lo), y: 4, z: 8, core: 2. Of those that a mesh axis runs over, the one named last changes fastest.
Arguments:
- tokens: bfloat16 [32, 1024, 2240], P('dp', 'seq'), may hold values from -8 to 8
- q_raw: bfloat16 [32, 1024, 1120], P('dp', 'seq'), may hold values from -6 to 6
- k_raw: bfloat16 [32, 1024, 1120], P('dp', 'seq'), may hold values from -6 to 6
- w_value: bfloat16 [2240, 1120], P('dp'), may hold values from -0.125 to 0.125
- w_out: bfloat16 [1120, 2240], P('dp'), may hold values from -0.1875 to 0.1875
- cotangent: bfloat16 [32, 1024, 2240], P('dp', 'seq'), may hold values from -6 to 6
Outputs:
- att_output: bfloat16 [32, 1024, 2240], P('dp', 'seq')
- grad_tokens: bfloat16 [32, 1024, 2240], P('dp', 'seq')
- grad_query: bfloat16 [32, 1024, 1120], P('dp', 'seq')
- grad_key: bfloat16 [32, 1024, 1120], P('dp', 'seq')
- grad_value_w: float32 [2240, 1120], P('dp', 'seq')
- grad_out_w: float32 [1120, 2240], P('dp', 'seq')
All inputs are finite; a program needn't handle non-finite values.
Results may differ from a plain program's by a relative error of at most 0.005.
Values may be sent and summed in bfloat16 or wider, within the bound.
A program may use at most 128 MiB of HBM per device.

v0:
```python
import jax
import jax.numpy as jnp
from jax import lax
from jax.sharding import PartitionSpec as P

HEADS = 35
HS = 32


def body(tokens, q_raw, k_raw, w_value, w_out, cotangent):
    high = lax.Precision.HIGHEST
    images, tok_count, feat_width = tokens.shape
    head_width = q_raw.shape[2]
    cot_cols = lax.all_to_all(cotangent, "seq", split_axis=2, concat_axis=1, tiled=True)
    value_full = lax.all_gather(w_value, "dp", axis=0, tiled=True)
    flat_rows = tokens.reshape(images * tok_count, feat_width)
    values = jnp.dot(flat_rows, value_full, preferred_element_type=jnp.float32).astype(jnp.bfloat16)
    values_heads = values.reshape(images, tok_count, HEADS, HS)
    key_heads = jnp.maximum(k_raw, 0).reshape(images, tok_count, HEADS, HS)
    local_state = jnp.einsum(
        "bnhd,bnhe->bhde", key_heads, values_heads, preferred_element_type=jnp.float32
    )
    feat_key = key_heads.astype(jnp.float32)
    local_total = jnp.sum(feat_key, axis=1)
    kv_state, key_total = lax.psum((local_state, local_total), "seq")
    out_full = lax.all_gather(w_out, "dp", axis=0, tiled=True)
    feat_query = jnp.maximum(q_raw, 0).astype(jnp.float32).reshape(images, tok_count, HEADS, HS)
    numer = jnp.einsum("bnhd,bhde->bnhe", feat_query, kv_state, precision=high)
    denom = jnp.einsum("bnhd,bhd->bnh", feat_query, key_total, precision=high) + 1.0
    att_ratio = numer / denom[..., None]
    att_heads = att_ratio.astype(jnp.bfloat16).reshape(images * tok_count, head_width)
    att_output = jnp.dot(att_heads, out_full, preferred_element_type=jnp.float32).astype(
        jnp.bfloat16
    )
    cot_rows = cotangent.reshape(images * tok_count, feat_width)
    grad_heads = lax.dot_general(
        cot_rows, out_full, (((1,), (1,)), ((), ())), preferred_element_type=jnp.float32
    )
    grad_numer = grad_heads.reshape(images, tok_count, HEADS, HS) / denom[..., None]
    grad_denom = -jnp.sum(grad_numer * att_ratio, axis=-1)
    query_part = jnp.einsum("bnhe,bhde->bnhd", grad_numer, kv_state, precision=high)
    query_part = query_part + grad_denom[..., None] * key_total[:, None]
    grad_query = jnp.where(
        q_raw > 0, query_part.reshape(images, tok_count, head_width), 0.0
    ).astype(jnp.bfloat16)
    local_gstate = jnp.einsum("bnhd,bnhe->bhde", feat_query, grad_numer, precision=high)
    local_gtotal = jnp.einsum("bnhd,bnh->bhd", feat_query, grad_denom, precision=high)
    grad_state, grad_total = lax.psum((local_gstate, local_gtotal), "seq")
    grad_values = jnp.einsum("bnhd,bhde->bnhe", feat_key, grad_state, precision=high).astype(
        jnp.bfloat16
    )
    values_f = values_heads.astype(jnp.float32)
    key_part = (
        jnp.einsum("bnhe,bhde->bnhd", values_f, grad_state, precision=high) + grad_total[:, None]
    )
    grad_key = jnp.where(k_raw > 0, key_part.reshape(images, tok_count, head_width), 0.0).astype(
        jnp.bfloat16
    )
    grad_flat = grad_values.reshape(images, tok_count, head_width)
    grad_rows = grad_flat.reshape(images * tok_count, head_width)
    grad_tokens = lax.dot_general(
        grad_rows, value_full, (((1,), (1,)), ((), ())), preferred_element_type=jnp.float32
    )
    value_cols = lax.all_to_all(grad_flat, "seq", split_axis=2, concat_axis=1, tiled=True)
    value_term = jnp.einsum(
        "bnd,bne->de",
        lax.all_gather(tokens, "seq", axis=1, tiled=True),
        value_cols,
        preferred_element_type=jnp.float32,
    )
    heads_seq = att_heads.reshape(images, tok_count, head_width)
    out_term = jnp.einsum(
        "bnd,bne->de",
        lax.all_gather(heads_seq, "seq", axis=1, tiled=True),
        cot_cols,
        preferred_element_type=jnp.float32,
    )
    grad_value_w, grad_out_w = (
        lax.psum_scatter(value_term, "dp", scatter_dimension=0, tiled=True),
        lax.psum_scatter(out_term, "dp", scatter_dimension=0, tiled=True),
    )
    return (
        att_output.reshape(images, tok_count, feat_width),
        grad_tokens.astype(jnp.bfloat16).reshape(images, tok_count, feat_width),
        grad_query,
        grad_key,
        grad_value_w,
        grad_out_w,
    )


def solution(mesh):
    return jax.shard_map(
        body,
        mesh=mesh,
        in_specs=(
            P("dp", "seq", None),
            P("dp", "seq", None),
            P("dp", "seq", None),
            P("dp", None),
            P("dp", None),
            P("dp", "seq", None),
        ),
        out_specs=(
            P("dp", "seq", None),
            P("dp", "seq", None),
            P("dp", "seq", None),
            P("dp", "seq", None),
            P("dp", "seq"),
            P("dp", "seq"),
        ),
        check_vma=False,
    )
```

profile of v0, /device:TPU:1, one launch (start us, length us, event | category | flops | bytes accessed | tf_op | source)
XLA Modules:
  0.0 667.1 jit_solution(14526017426088755007)
XLA Ops:
  10.6 53.4 %psum.29 = f32[2,35,32]{2,1,0:T(8,128)S(1)} all-reduce(f32[2,35,32]{2,1,0:T(8,128)S(1)} %reduce_sum.21), channel_id=1, replica_groups=mesh['dp'=16,'seq'=16] {'seq'}, use_global_device_ids=true, to_apply=%region_2.0 | all-reduce | flops 2240 | bytes 17920 | tf_op jit(solution)/shard_map/psum | solution.py:25
  64.8 55.6 %all-gather.11.cloned.1.call-done = bf16[16,140,1120]{2,1,0:T(8,128)(2,1)} async-done(((bf16[1,140,1120]{2,1,0:T(8,128)(2,1)}), bf16[16,140,1120]{2,1,0:T(8,128)(2,1)}) %all-gather.11.cloned.1.call-update) | async-done | bytes 5017616 | tf_op jit(solution)/shard_map/all_gather | solution.py:15
  120.4 7.8 %reshape.65 = bf16[2240,1120]{1,0:T(8,128)(2,1)} reshape(bf16[16,140,1120]{2,1,0:T(8,128)(2,1)} %all-gather.11.cloned.1.call-done) | data formatting | bytes 10035200
  128.2 5.3 convolution_convert_fusion.2
  134.8 93.2 %all-gather.13.cloned.1.call-done = bf16[16,70,2240]{2,1,0:T(8,128)(2,1)} async-done(((bf16[1,70,2240]{2,1,0:T(8,128)(2,1)}), bf16[16,70,2240]{2,1,0:T(8,128)(2,1)}) %all-gather.13.cloned.1.call-update) | async-done | bytes 5017616 | tf_op jit(solution)/shard_map/all_gather | solution.py:26
  228.0 6.4 dot_general.51
  234.4 3.6 fusion.7
  242.2 129.2 %all-reduce.9.cloned.1.call-done = (f32[2,35,32,32]{3,2,1,0:T(8,128)}, f32[2,35,32,32]{3,2,1,0:T(8,128)}) async-done(((f32[2,35,32,32]{3,2,1,0:T(8,128)}, f32[2,35,32,32]{3,2,1,0:T(8,128)}), (f32[2,35,32,32]{3,2,1,0:T(8,128)}, f32[2,35,32,32]{3,2,1,0:T(8,128)})) %all-reduce.9.cloned.1.call-update) | async-done | bytes 573456 | tf_op jit(solution)/shard_map/psum | solution.py:25
  371.4 3.4 multiply_reduce_fusion
  378.0 3.9 reshape.83
  381.9 5.9 all-to-all-start.1
  389.7 15.1 %all-to-all-done.1 = bf16[16,2,8960]{2,1,0:T(2,128)(2,1)S(1)} async-done(((bf16[16,2,8960]{2,1,0:T(2,128)(2,1)}), bf16[16,2,8960]{2,1,0:T(2,128)(2,1)S(1)}, u32[]{:S(2)}, u32[]{:S(2)}) %all-to-all-start.1) | async-done | bytes 573472 | tf_op jit(solution)/shard_map/all_to_all | solution.py:14
  409.0 2.9 all_to_all.33
  411.9 6.5 reshape.67
  420.0 4.8 convolution_convert_fusion.1
  429.0 4.1 convolution_convert_fusion
  434.2 3.0 fusion.4
  439.3 4.4 copy.103
  444.8 4.2 all-to-all-start
  449.1 52.6 %psum.31 = f32[2,35,32]{2,1,0:T(8,128)S(1)} all-reduce(f32[2,35,32]{2,1,0:T(8,128)S(1)} %bitcast.133), channel_id=1, replica_groups=mesh['dp'=16,'seq'=16] {'seq'}, use_global_device_ids=true, to_apply=%region_5.6 | all-reduce | flops 2240 | bytes 17920 | tf_op jit(solution)/shard_map/psum | solution.py:48
  504.6 6.3 convolution_bitcast_fusion
  511.0 3.8 convolution_bitcast_fusion.1
  514.8 44.4 %fusion = f32[72,140]{1,0:T(8,128)S(1)} fusion(f32[1120,140]{1,0:T(8,128)S(1)} %convolution_bitcast_fusion.1), kind=kCustom, calls=%all-reduce-scatter | all-reduce-scatter fusion | flops 161281 | bytes 668544
  560.5 97.2 %all-reduce.7.cloned.1.call-done = f32[2240,70]{0,1:T(8,128)} async-done(((f32[2240,70]{0,1:T(8,128)}), f32[2240,70]{0,1:T(8,128)}) %all-reduce.7.cloned.1.call-update) | async-done | bytes 627216
  (81 shorter events, 34.4 us)
Async XLA Ops:
  7.2 2.8 copy-start.9
  7.2 113.2 %all-gather.11.cloned.1.call-start = ((), (), s32[]{:S(2)}) async-start(), calls=%async_computation.4 | async-start | bytes 5640192 | tf_op jit(solution)/shard_map/all_gather | solution.py:15
  7.9 220.1 %all-gather.13.cloned.1.call-start = ((), (), s32[]{:S(2)}) async-start(), calls=%async_computation.5 | async-start | bytes 5640192 | tf_op jit(solution)/shard_map/all_gather | solution.py:26
  8.7 362.7 %all-reduce.9.cloned.1.call-start = ((), (), s32[]{:S(2)}) async-start(), calls=%async_computation.7 | async-start | bytes 4587520 | tf_op jit(solution)/shard_map/psum | solution.py:25
  64.1 173.9 %copy-start.3 = (bf16[2,64,1120]{1,2,0:T(8,128)(2,1)}, bf16[2,64,1120]{1,2,0:T(8,128)(2,1)S(1)}, u32[]{:S(2)}) copy-start(bf16[2,64,1120]{1,2,0:T(8,128)(2,1)S(1)} %broadcast_maximum_fusion) | copy-start | bytes 860164
  64.7 63.5 %copy-start.2 = (bf16[2,64,2240]{2,1,0:T(8,128)(2,1)S(1)}, bf16[2,64,2240]{2,1,0:T(8,128)(2,1)}, u32[]{:S(2)}) copy-start(bf16[2,64,2240]{2,1,0:T(8,128)(2,1)} %param.6) | copy-start | bytes 1720324
  134.8 99.6 %copy-start.6 = (bf16[2,64,2240]{2,1,0:T(8,128)(2,1)S(1)}, bf16[2,64,2240]{2,1,0:T(8,128)(2,1)}, u32[]{:S(2)}) copy-start(bf16[2,64,2240]{2,1,0:T(8,128)(2,1)} %param.11) | copy-start | bytes 1720324
  238.0 2.1 copy-start.1
  241.6 129.8 %copy-start.4 = (bf16[2,64,1120]{1,2,0:T(8,128)(2,1)S(1)}, bf16[2,64,1120]{1,2,0:T(8,128)(2,1)}, u32[]{:S(2)}) copy-start(bf16[2,64,1120]{1,2,0:T(8,128)(2,1)} %copy-done.3) | copy-start | bytes 860164
  241.6 263.0 %all-gather.7.cloned.1.call-start = ((), (), s32[]{:S(2)}) async-start(), calls=%async_computation.2 | async-start | bytes 10027008 | tf_op jit(solution)/shard_map/all_gather | solution.py:67
  242.2 268.8 %all-gather.9.cloned.1.call-start = ((), (), s32[]{:S(2)}) async-start(), calls=%async_computation.3 | async-start | bytes 5013504 | tf_op jit(solution)/shard_map/all_gather | solution.py:74
  374.8 1.1 copy-start.7
  378.0 9.8 %copy-start.11 = (u32[256]{0:T(256)S(1)}, u32[256]{0:T(256)}, u32[]{:S(2)}) copy-start(u32[256]{0:T(256)} %constant.14) | copy-start | bytes 3076
  381.9 22.9 %all-to-all-start.1 = ((bf16[16,2,8960]{2,1,0:T(2,128)(2,1)}), bf16[16,2,8960]{2,1,0:T(2,128)(2,1)S(1)}, u32[]{:S(2)}, u32[]{:S(2)}) async-start(bf16[16,2,8960]{2,1,0:T(2,128)(2,1)} %reshape.83), calls=%async_computation.1 | async-start | bytes 1146880 | tf_op jit(solution)/shard_map/all_to_all | solution.py:14
  433.1 1.1 copy-start.10
  437.1 1.2 copy-start.5
  439.3 62.3 %copy-start = (f32[2,35,32,32]{3,2,1,0:T(8,128)S(1)}, f32[2,35,32,32]{3,2,1,0:T(8,128)}, u32[]{:S(2)}) copy-start(f32[2,35,32,32]{3,2,1,0:T(8,128)} %get-tuple-element.25) | copy-start | bytes 860164
  444.8 58.9 %all-to-all-start = ((bf16[16,2,4480]{2,1,0:T(2,128)(2,1)}), bf16[16,2,4480]{2,1,0:T(2,128)(2,1)S(1)}, u32[]{:S(2)}, u32[]{:S(2)}) async-start(bf16[16,2,4480]{2,1,0:T(2,128)(2,1)} %reshape.81), calls=%async_computation | async-start | bytes 573440 | tf_op jit(solution)/shard_map/all_to_all | solution.py:64
  449.1 208.6 %all-reduce.7.cloned.1.call-start = ((), (), s32[]{:S(2)}) async-start(), calls=%async_computation.6 | async-start | bytes 1327104
  504.6 6.4 copy-start.8
  559.2 100.2 %collective-permute-start = (f32[30,140]{1,0:T(8,128)S(1)}, f32[30,140]{1,0:T(8,128)S(1)}, u32[]{:S(2)}, u32[]{:S(2)}) collective-permute-start(f32[30,140]{1,0:T(8,128)S(1)} %slice), channel_id=1, source_target_pairs={{0,16},{16,32},{32,48},{48,64},{64,80},{80,96},{96,112},{112,128},... | collective-permute-start | bytes 50408
Sparse Core Ops, SparseCore 0:
  10.6 109.7 all-gather.10
  123.0 104.9 all-gather.12
  241.7 129.6 all-reduce.8
  373.1 67.2 all-gather.6
  442.0 42.2 all-gather.8
  511.1 146.5 all-reduce.6
where the time goes:
time: 678 us; the launch traced here: 667 us
  waiting for transfers between devices  392 us (58%)
  blocking collectives  150 us (22%)
  local copies, waits for them, and re-layouts  53.7 us (8%)
  matrix products  42.4 us (6%)
  between operations  15.7 us (2%)
  starting transfers between devices  11.7 us (2%)
    psum x1, waiting for transfers between devices, body(): kv_state, key_total = lax.psum((local_state, local_total), 'seq')  129 us
    unnamed x8, waiting for transfers between devices  99.1 us
    all_gather x1, waiting for transfers between devices, body(): out_full = lax.all_gather(w_out, 'dp', axis=0, tiled=True)  93.2 us
    all_gather x1, waiting for transfers between devices, body(): value_full = lax.all_gather(w_value, 'dp', axis=0, tiled=True)  55.6 us
    psum x1, blocking collectives, body(): kv_state, key_total = lax.psum((local_state, local_total), 'seq')  53.4 us
    psum x1, blocking collectives, body(): grad_state, grad_total = lax.psum((local_gstate, local_gtotal), 'seq')  52.6 us
    unnamed x1, blocking collectives  44.4 us
    unnamed x41, local copies, waits for them, and re-layouts  30.2 us
  transfers between devices with their start and end apart: 9, of which 5 were waited for; matrix products, arithmetic and copies ran while one was open for 19% of the time, Pallas kernels for 0%

commit v1 on v0

v1 whole, which is shorter than its diff:
```python
import jax
import jax.numpy as jnp
from jax import lax
from jax.experimental import pallas as pl
from jax.experimental.pallas import tpu as pltpu
from jax.sharding import PartitionSpec as P

BF = jnp.bfloat16
F32 = jnp.float32
MESH = pl.DeviceIdType.MESH
VM = pltpu.VMEM
SIZE = {"x": 4, "y": 4, "z": 8}
ORDERS = (("x", "y", "z"), ("y", "z", "x"), ("z", "x", "y"))
PAIRS = ((0, 1), (1, 0), (1, 1), (2, 0), (2, 1), (3, 0), (3, 1))
N_SEMS = 320


class Place:
    def __init__(self):
        dp = lax.axis_index("dp")
        seq = lax.axis_index("seq")
        self.z = lax.rem(dp, 8)
        self.y = lax.div(seq, 4)
        self.xl = lax.rem(lax.div(seq, 2), 2)
        self.c = lax.rem(seq, 2)
        self.x = lax.div(dp, 8) * 2 + self.xl
        self.p = self.y * 2 + self.xl

    def step(self, d, k):
        return lax.rem(getattr(self, d) + (k % SIZE[d]), SIZE[d])

    def dev(self, x=None, y=None, z=None, c=None):
        x = self.x if x is None else x
        y = self.y if y is None else y
        z = self.z if z is None else z
        c = self.c if c is None else c
        return (lax.div(x, 2) * 8 + z, (y * 2 + lax.rem(x, 2)) * 2 + c)

    def peer(self, d, k):
        return self.dev(**{d: self.step(d, k)})

    def sibling(self):
        return self.dev(c=1 - self.c)

    def row_peer(self, dy, dx):
        xl = lax.rem(self.xl + dx, 2)
        return self.dev(y=self.step("y", dy), x=self.x - self.xl + xl)

    def index(self, o, open_, d, b, half=None):
        co = {"x": self.x, "y": self.y, "z": self.z}
        for e in open_:
            co[e] = None
        co[d] = b
        every = slice(None)
        x = co["x"]
        xh, xl = (every, every) if x is None else (lax.div(x, 2), lax.rem(x, 2))
        z = every if co["z"] is None else co["z"]
        y = every if co["y"] is None else co["y"]
        out = (xh, z, y, xl, o)
        return out if half is None else out + (half,)


class Wire:
    def __init__(self, sems):
        self.sems = sems
        self.started = []

    def send(self, src, dst, dev):
        k = len(self.started)
        cp = pltpu.make_async_remote_copy(
            src_ref=src,
            dst_ref=dst,
            send_sem=self.sems.at[0, k],
            recv_sem=self.sems.at[1, k],
            device_id=dev,
            device_id_type=MESH,
        )
        cp.start()
        self.started.append(cp)
        return cp

    def drain(self):
        for cp in self.started:
            cp.wait_send()


def gather(wire, me, buf, o):
    open_ = []
    sib = []

    def piece(d, b, half=None):
        return buf.at[(me.c,) + me.index(o, open_, d, b, half)]

    def share(d, b, half=None):
        ref = piece(d, b, half)
        sib.append(wire.send(ref, ref, me.sibling()))

    for n, d in enumerate(ORDERS[o]):
        last = n == 2
        if last:
            share(d, getattr(me, d))
        if d != "z":
            own = piece(d, getattr(me, d))
            cps = [wire.send(own, own, me.peer(d, k)) for k in range(1, SIZE[d])]
            yield
            for k, cp in enumerate(cps, 1):
                cp.wait_recv()
                if last:
                    share(d, me.step(d, -k))
        else:
            for s in range(1, 5):
                hp, hm = (0, 1) if s == 4 else (None, None)
                fp = piece(d, me.step(d, -(s - 1)), hp)
                fm = piece(d, me.step(d, s - 1), hm)
                plus = wire.send(fp, fp, me.peer(d, 1))
                minus = wire.send(fm, fm, me.peer(d, -1))
                yield
                plus.wait_recv()
                minus.wait_recv()
                if last:
                    share(d, me.step(d, -s), hp)
                    share(d, me.step(d, s), hm)
        open_.append(d)
    yield
    for cp in sib:
        cp.wait_recv()


def scatter(wire, me, buf, o, rx, fin):
    rx = iter(rx)
    dims = ORDERS[o]
    for n, d in enumerate(dims):
        open_ = dims[n + 1 :]
        last = n == 2

        def at(k, half=None):
            return me.index(o, open_, d, me.step(d, k), half)

        own = at(0)
        if d != "z":
            slots = [next(rx) for _ in range(3)]
            cps = [
                wire.send(buf.at[at(k)], slots[k - 1], me.peer(d, k)) for k in (1, 2, 3)
            ]
            yield
            acc = buf[own].astype(F32)
            for k in range(3):
                cps[k].wait_recv()
                acc = acc + slots[k][...].astype(F32)
        else:
            up = [next(rx) for _ in range(4)]
            down = [next(rx) for _ in range(4)]
            for s in range(1, 5):
                k = 5 - s
                hp, hm = (0, 1) if s == 1 else (None, None)
                if s > 1:
                    plus.wait_recv()
                    minus.wait_recv()
                    for sign, slot, half in ((1, up[s - 2], 0), (-1, down[s - 2], 1)):
                        i = at(sign * k, half if s == 2 else None)
                        buf[i] = (buf[i].astype(F32) + slot[...].astype(F32)).astype(BF)
                plus = wire.send(buf.at[at(k, hp)], up[s - 1], me.peer(d, 1))
                minus = wire.send(buf.at[at(-k, hm)], down[s - 1], me.peer(d, -1))
                yield
            plus.wait_recv()
            minus.wait_recv()
            acc = buf[own].astype(F32) + up[3][...].astype(F32) + down[3][...].astype(F32)
        if last:
            fin[me.c, me.p, o] = acc
        else:
            buf[own] = acc.astype(BF)


def scatter_slots(o):
    dims = ORDERS[o]
    out = []
    for n, d in enumerate(dims):
        open_ = dims[n + 1 :]
        shape = ()
        if "x" in open_:
            shape += (2,)
        if "z" in open_:
            shape += (8,)
        if "y" in open_:
            shape += (4,)
        if "x" in open_:
            shape += (2,)
        tile = (16, 128)
        if d != "z":
            out += [VM(shape + (2,) + tile, BF)] * 3
        else:
            out += ([VM(shape + tile, BF)] + [VM(shape + (2,) + tile, BF)] * 3) * 2
    return out


def spread(wire, me, fin):
    mine = fin.at[me.c, me.p]
    cps = [wire.send(mine, mine, me.row_peer(dy, dx)) for dy, dx in PAIRS]
    yield
    for cp in cps:
        cp.wait_recv()
    half = fin.at[me.c]
    cp = wire.send(half, half, me.sibling())
    yield
    cp.wait_recv()


def seq_sum(wire, me, part, from_sib, from_row, total):
    cp = wire.send(part.at[1 - me.c], from_sib, me.sibling())
    yield
    cp.wait_recv()
    part[me.c] = part[me.c] + from_sib[...]
    cps = []
    for n, (dy, dx) in enumerate(PAIRS):
        p = me.step("y", dy) * 2 + lax.rem(me.xl + dx, 2)
        cps.append(
            wire.send(part.at[me.c, pl.ds(6 * p, 6)], from_row.at[n], me.row_peer(dy, dx))
        )
    yield
    acc = part[me.c, pl.ds(6 * me.p, 6)]
    for n, cp in enumerate(cps):
        cp.wait_recv()
        acc = acc + from_row[n]
    total[me.c, pl.ds(6 * me.p, 6)] = acc
    mine = total.at[me.c, pl.ds(6 * me.p, 6)]
    cps = [wire.send(mine, mine, me.row_peer(dy, dx)) for dy, dx in PAIRS]
    yield
    for cp in cps:
        cp.wait_recv()
    half = total.at[me.c]
    cp = wire.send(half, half, me.sibling())
    yield
    cp.wait_recv()


def step(gens):
    for g in list(gens):
        try:
            next(g)
        except StopIteration:
            gens.remove(g)


def split(a):
    hi = a.astype(BF)
    return hi, (a - hi.astype(F32)).astype(BF)


def dot(a, b):
    return jnp.dot(a, b, preferred_element_type=F32)


def dot_t(a, b):
    return lax.dot_general(a, b, (((1,), (1,)), ((), ())), preferred_element_type=F32)


def t_dot(a, b):
    return lax.dot_general(a, b, (((0,), (0,)), ((), ())), preferred_element_type=F32)


def fold(m):
    return m[0:32] + m[32:64] + m[64:96] + m[96:128]


def kernel(
    tok, q_in, k_in, wv_in, wo_in, cot,
    out_o, gtok_o, gq_o, gk_o, gwv_o, gwo_o,
    sems, wv, wo, wvp, wop, tokp, tok_t, cotp, qp, kp, val, attf, denf, att_h, att_p, att_t,
    ghp, gvp, gqp, gkp, part1, part2, sib1, sib2, row1, row2, tot1, tot2,
    rs_v, rs_o, fin_v, fin_o, *slots,
):
    me = Place()
    wire = Wire(sems)
    per = [len(scatter_slots(o)) for o in range(3)]
    cut = [0]
    for n in per * 2:
        cut.append(cut[-1] + n)
    slot_sets = [slots[cut[i] : cut[i + 1]] for i in range(6)]

    wvp[...] = jnp.zeros_like(wvp)
    wvp[0:140, 0:1120] = wv_in[...]
    wop[...] = jnp.zeros_like(wop)
    wop[0:70, 0:2240] = wo_in[...]
    xh = lax.div(me.x, 2)
    for k in range(6):
        t = 6 * me.p + k
        r, l = lax.rem(t, 9), lax.div(t, 9)
        wv[me.c, xh, me.z, me.y, me.xl, k // 2, k % 2] = wvp[
            pl.ds(pl.multiple_of(r * 16, 16), 16),
            pl.ds(pl.multiple_of((5 * me.c + l) * 128, 128), 128),
        ]
        r, l = lax.rem(t, 5), lax.div(t, 5)
        wo[me.c, xh, me.z, me.y, me.xl, k // 2, k % 2] = wop[
            pl.ds(pl.multiple_of(r * 16, 16), 16),
            pl.ds(pl.multiple_of((9 * me.c + l) * 128, 128), 128),
        ]

    peers = [me.peer("x", k) for k in (1, 2, 3)] + [me.peer("y", k) for k in (1, 2, 3)]
    peers += [me.peer("z", 1), me.peer("z", -1), me.sibling()]
    peers += [me.row_peer(dy, 1) for dy in (1, 2, 3)]
    barrier = pltpu.get_barrier_semaphore()
    for dev in peers:
        pl.semaphore_signal(barrier, inc=1, device_id=dev, device_id_type=MESH)
    pl.semaphore_wait(barrier, len(peers))

    ga = [gather(wire, me, wv, o) for o in range(3)]
    gb = [gather(wire, me, wo, o) for o in range(3)]
    step(ga)

    tokp[...] = jnp.zeros_like(tokp)
    for i in range(16):
        tokp[:, 144 * i : 144 * i + 140] = tok[:, 140 * i : 140 * i + 140]
    step(ga)
    qp[...] = jnp.zeros_like(qp)
    qp[:, 0:1120] = q_in[...]
    kp[...] = jnp.zeros_like(kp)
    kp[:, 0:1120] = k_in[...]
    step(ga)
    step(gb)
    cotp[me.c] = jnp.zeros((128, 2304), BF)
    cotp[me.c, :, 0:2240] = cot[...]
    ex_cot = wire.send(cotp.at[me.c], cotp.at[me.c], me.sibling())
    for i in range(9):
        tok_t[me.c, 256 * i : 256 * i + 256] = tokp[:, 256 * i : 256 * i + 256].T
    ex_tok = wire.send(tok_t.at[me.c], tok_t.at[me.c], me.sibling())
    part1[...] = jnp.zeros_like(part1)
    part2[...] = jnp.zeros_like(part2)
    att_p[...] = jnp.zeros_like(att_p)
    gvp[me.c] = jnp.zeros((128, 1280), BF)
    rsv_t = rs_v.reshape(16, 48, 16, 128)
    rso_t = rs_o.reshape(16, 48, 16, 128)
    rsv_t[:, 45:48] = jnp.zeros((16, 3, 16, 128), BF)
    rso_t[:, 45:48] = jnp.zeros((16, 3, 16, 128), BF)
    while ga:
        step(ga)
        step(gb)

    wv_t = wv.reshape(2, 16, 48, 16, 128)
    wo_t = wo.reshape(2, 16, 48, 16, 128)
    row = lax.broadcasted_iota(jnp.int32, (128, 128), 0) // 32
    col = lax.broadcasted_iota(jnp.int32, (128, 128), 1) // 32
    heads = (row == col).astype(F32)
    heads_b = heads.astype(BF)

    for group in ((0, 1), (2, 3), (4,), (5, 6), (7, 8)):
        acc = None
        for h in range(2):
            slab = jnp.concatenate(
                [
                    wv_t[s // 5, 8 * h : 8 * h + 8, 9 * (s % 5) : 9 * (s % 5) + 9].reshape(1152, 128)
                    for s in group
                ],
                axis=1,
            )
            part = dot(tokp[:, 1152 * h : 1152 * h + 1152], slab)
            acc = part if acc is None else acc + part
        val[:, 128 * group[0] : 128 * (group[-1] + 1)] = acc.astype(BF)

    def lanes_of(g):
        return pl.ds(pl.multiple_of(g * 128, 128), 128)

    def put(ref, img, g, m, line):
        ref[img, pl.ds(5 * g, 4)] = fold(m * heads).reshape(4, 8, 128)
        ref[img, 5 * g + 4] = jnp.broadcast_to(line, (8, 128))

    def take(ref, img, g):
        m = ref[img, pl.ds(5 * g, 4)].reshape(32, 128)
        m = jnp.concatenate([m, m, m, m], axis=0) * heads
        return m, ref[img, 5 * g + 4][0:1]

    for img in range(2):
        rows = slice(64 * img, 64 * img + 64)

        def state(g, carry, img=img, rows=rows):
            ln = lanes_of(g)
            kf = jnp.maximum(kp[rows, ln], 0)
            line = jnp.sum(kf.astype(F32), axis=0, keepdims=True)
            put(part1, img, g, t_dot(kf, val[rows, ln]), line)
            return carry

        lax.fori_loop(0, 9, state, 0)

    s1 = [seq_sum(wire, me, part1, sib1, row1, tot1)]
    while s1:
        step(s1)
        step(gb)

    for img in range(2):
        rows = slice(64 * img, 64 * img + 64)

        def attend(g, carry, img=img, rows=rows):
            ln = lanes_of(g)
            qf = jnp.maximum(qp[rows, ln], 0)
            kv, kt = take(tot1, img, g)
            hi, lo = split(kv)
            numer = dot(qf, hi) + dot(qf, lo)
            hi, lo = split(qf.astype(F32) * kt)
            denom = dot(hi, heads_b) + dot(lo, heads_b) + 1.0
            ratio = numer / denom
            denf[rows, ln] = denom
            attf[rows, ln] = ratio
            att_h[rows, ln] = ratio.astype(BF)
            return carry

        lax.fori_loop(0, 9, attend, 0)
    for i in range(16):
        att_p[:, 80 * i : 80 * i + 70] = att_h[:, 70 * i : 70 * i + 70]
    for i in range(5):
        att_t[me.c, 256 * i : 256 * i + 256] = att_p[:, 256 * i : 256 * i + 256].T
    ex_att = wire.send(att_t.at[me.c], att_t.at[me.c], me.sibling())

    while gb:
        step(gb)

    def out_rows(i, n):
        return jnp.concatenate(
            [
                wo_t[s // 9, i : i + n, 5 * (s % 9) : 5 * (s % 9) + 5].reshape(80 * n, 128)
                for s in range(18)
            ],
            axis=1,
        )

    ghp[...] = jnp.zeros_like(ghp)
    for i in range(4):
        gh = dot_t(cotp[me.c], out_rows(4 * i, 4))
        for j in range(4):
            at = 70 * (4 * i + j)
            ghp[:, at : at + 70] = gh[:, 80 * j : 80 * j + 70]

    for img in range(2):
        rows = slice(64 * img, 64 * img + 64)

        def grads(g, carry, img=img, rows=rows):
            ln = lanes_of(g)
            q = qp[rows, ln]
            qf = jnp.maximum(q, 0)
            kv, kt = take(tot1, img, g)
            kv_hi, kv_lo = split(kv)
            gn = ghp[rows, ln] / denf[rows, ln]
            hi, lo = split(gn * attf[rows, ln])
            gd = -(dot(hi, heads_b) + dot(lo, heads_b))
            hi, lo = split(gn)
            part = dot_t(hi, kv_hi) + dot_t(lo, kv_hi) + dot_t(hi, kv_lo) + gd * kt
            gqp[rows, ln] = jnp.where(q > 0, part, 0.0).astype(BF)
            line = jnp.sum(qf.astype(F32) * gd, axis=0, keepdims=True)
            put(part2, img, g, t_dot(qf, hi) + t_dot(qf, lo), line)
            return carry

        lax.fori_loop(0, 9, grads, 0)

    s2 = [seq_sum(wire, me, part2, sib2, row2, tot2)]
    step(s2)
    gq_o[...] = gqp[:, 0:1120]
    ex_cot.wait_recv()
    ex_att.wait_recv()
    step(s2)

    cot_half = pl.ds(pl.multiple_of(me.c * 1152, 128), 1152)

    def out_term(i, carry):
        a = jnp.concatenate([att_t[s, pl.ds(pl.multiple_of(160 * i, 32), 160)] for s in (0, 1)], axis=1)
        b = jnp.concatenate([cotp[0, :, cot_half], cotp[1, :, cot_half]], axis=0)
        m = dot(a, b).astype(BF)
        for l in range(9):
            rso_t[pl.ds(2 * i, 2), 5 * l : 5 * l + 5] = m[:, 128 * l : 128 * l + 128].reshape(2, 5, 16, 128)
        return carry

    lax.fori_loop(0, 8, out_term, 0)
    step(s2)
    so = [scatter(wire, me, rs_o, o, slot_sets[o], fin_o) for o in range(3)]
    step(so)
    for i in range(9):
        slab = jnp.concatenate(
            [
                wo_t[s // 9, :, 5 * (s % 9) : 5 * (s % 9) + 5].reshape(1280, 128)
                for s in (2 * i, 2 * i + 1)
            ],
            axis=1,
        )
        width = min(256, 2240 - 256 * i)
        out_o[:, 256 * i : 256 * i + width] = dot(att_p[...], slab).astype(BF)[:, 0:width]
    while s2:
        step(s2)

    for img in range(2):
        rows = slice(64 * img, 64 * img + 64)

        def last_grads(g, carry, img=img, rows=rows):
            ln = lanes_of(g)
            k = kp[rows, ln]
            kf = jnp.maximum(k, 0)
            gs, gt = take(tot2, img, g)
            hi, lo = split(gs)
            gvp[me.c, rows, ln] = (dot(kf, hi) + dot(kf, lo)).astype(BF)
            v = val[rows, ln]
            part = dot_t(v, hi) + dot_t(v, lo) + gt
            gkp[rows, ln] = jnp.where(k > 0, part, 0.0).astype(BF)
            return carry

        lax.fori_loop(0, 9, last_grads, 0)
    ex_gv = wire.send(gvp.at[me.c], gvp.at[me.c], me.sibling())
    step(so)
    gk_o[...] = gkp[:, 0:1120]
    ex_tok.wait_recv()
    ex_gv.wait_recv()

    gv_half = pl.ds(pl.multiple_of(me.c * 640, 128), 640)

    def value_term(i, carry):
        a = jnp.concatenate([tok_t[s, pl.ds(pl.multiple_of(288 * i, 32), 288)] for s in (0, 1)], axis=1)
        b = jnp.concatenate([gvp[0, :, gv_half], gvp[1, :, gv_half]], axis=0)
        m = dot(a, b).astype(BF)
        for l in range(5):
            rsv_t[pl.ds(2 * i, 2), 9 * l : 9 * l + 9] = m[:, 128 * l : 128 * l + 128].reshape(2, 9, 16, 128)
        return carry

    lax.fori_loop(0, 8, value_term, 0)
    sv = [scatter(wire, me, rs_v, o, slot_sets[3 + o], fin_v) for o in range(3)]
    step(sv)
    step(so)

    for i in range(4):
        w = jnp.concatenate(
            [
                wv_t[s // 5, 4 * i : 4 * i + 4, 9 * (s % 5) : 9 * (s % 5) + 9].reshape(576, 128)
                for s in range(9)
            ],
            axis=1,
        )
        gt = dot_t(gvp[me.c, :, 0:1152], w).astype(BF)
        for j in range(4):
            at = 140 * (4 * i + j)
            gtok_o[:, at : at + 140] = gt[:, 144 * j : 144 * j + 140]
        step(so)
    while sv:
        step(so)
        step(sv)
    while so:
        step(so)

    ends = [spread(wire, me, fin_o), spread(wire, me, fin_v)]
    while ends:
        step(ends)
    seq = me.p * 2 + me.c
    fin_vt = fin_v.reshape(2, 48, 16, 128)
    fin_ot = fin_o.reshape(2, 48, 16, 128)

    def slab_of(ref, s, per_core, height):
        tiles = ref[lax.div(s, per_core), pl.ds(lax.rem(s, per_core) * height, height)]
        return tiles.reshape(height * 16, 128)

    first = lax.div(70 * seq, 128)
    shift = 70 * seq - 128 * first
    m = jnp.concatenate([slab_of(fin_vt, jnp.minimum(first + j, 8), 5, 9) for j in range(2)], axis=1)
    gwv_o[...] = pltpu.roll(m, lax.rem(256 - shift, 256), 1)[0:140, 0:70]
    first = lax.div(140 * seq, 128)
    shift = 140 * seq - 128 * first
    m = jnp.concatenate([slab_of(fin_ot, jnp.minimum(first + j, 17), 9, 5) for j in range(3)], axis=1)
    gwo_o[...] = pltpu.roll(m, lax.rem(384 - shift, 384), 1)[0:70, 0:140]
    wire.drain()


def body(tokens, q_raw, k_raw, w_value, w_out, cotangent):
    shape = jax.ShapeDtypeStruct
    weight = VM((2, 2, 8, 4, 2, 3, 2, 16, 128), BF)
    partial = VM((2, 8, 4, 2, 3, 2, 16, 128), BF)
    state = VM((2, 48, 8, 128), F32)
    final = VM((2, 8, 3, 2, 16, 128), F32)
    slots = [s for _ in range(2) for o in range(3) for s in scatter_slots(o)]
    outs = pl.pallas_call(
        kernel,
        out_shape=(
            shape((128, 2240), BF),
            shape((128, 2240), BF),
            shape((128, 1120), BF),
            shape((128, 1120), BF),
            shape((140, 70), F32),
            shape((70, 140), F32),
        ),
        in_specs=[pl.BlockSpec(memory_space=VM)] * 6,
        out_specs=(pl.BlockSpec(memory_space=VM),) * 6,
        scratch_shapes=[
            pltpu.SemaphoreType.DMA((2, N_SEMS)),
            weight,
            weight,
            VM((144, 1408), BF),
            VM((80, 2432), BF),
            VM((128, 2304), BF),
            VM((2, 2304, 128), BF),
            VM((2, 128, 2304), BF),
            VM((128, 1152), BF),
            VM((128, 1152), BF),
            VM((128, 1152), BF),
            VM((128, 1152), F32),
            VM((128, 1152), F32),
            VM((128, 1152), BF),
            VM((128, 1280), BF),
            VM((2, 1280, 128), BF),
            VM((128, 1152), F32),
            VM((2, 128, 1280), BF),
            VM((128, 1152), BF),
            VM((128, 1152), BF),
            state,
            state,
            VM((48, 8, 128), F32),
            VM((48, 8, 128), F32),
            VM((7, 6, 8, 128), F32),
            VM((7, 6, 8, 128), F32),
            state,
            state,
            partial,
            partial,
            final,
            final,
            *slots,
        ],
        compiler_params=pltpu.CompilerParams(
            collective_id=0, has_side_effects=True, vmem_limit_bytes=60 * 2**20
        ),
    )(
        tokens.reshape(128, 2240),
        q_raw.reshape(128, 1120),
        k_raw.reshape(128, 1120),
        w_value,
        w_out,
        cotangent.reshape(128, 2240),
    )
    return (
        outs[0].reshape(2, 64, 2240),
        outs[1].reshape(2, 64, 2240),
        outs[2].reshape(2, 64, 1120),
        outs[3].reshape(2, 64, 1120),
        outs[4],
        outs[5],
    )


def solution(mesh):
    rows = P("dp", "seq", None)
    return jax.shard_map(
        body,
        mesh=mesh,
        in_specs=(rows, rows, rows, P("dp", None), P("dp", None), rows),
        out_specs=(rows, rows, rows, rows, P("dp", "seq"), P("dp", "seq")),
        check_vma=False,
    )
```

time: 678 us -> 180 us (0.27); the launches traced: 667 us -> 180 us
  waiting for transfers between devices: 392 us -> 0 us
  Pallas kernels: 0 us -> 173 us
  blocking collectives: 150 us -> 0 us
  local copies, waits for them, and re-layouts: 53.7 us -> 6.65 us
  matrix products: 42.4 us -> 0 us
  between operations: 15.7 us -> 0.66 us
  starting transfers between devices: 11.7 us -> 0 us
    pallas_call x0 -> x1, Pallas kernels: none -> 173 us  [body(): pl.pallas_call(kernel, out_shape=(shape((128, 2240), BF), shape((128, 224...]
    all_gather x4 -> x0, waiting for transfers between devices: 149 us -> none  [the longest x1 93.2 us: body(): out_full = lax.all_gather(w_out, 'dp', axis=0, tiled=True)]
    psum x1 -> x0, waiting for transfers between devices: 129 us -> none  [body(): kv_state, key_total = lax.psum((local_state, local_total), 'seq')]
    psum x2 -> x0, blocking collectives: 106 us -> none  [the longest x1 53.4 us: body(): kv_state, key_total = lax.psum((local_state, local_total), 'seq')]
    unnamed x8 -> x0, waiting for transfers between devices: 99.1 us -> none
    unnamed x1 -> x0, blocking collectives: 44.4 us -> none
    dot_general x14 -> x0, matrix products: 42.4 us -> none  [the longest x1 6.34 us: body(): jnp.einsum('bnd,bne->de', lax.all_gather(tokens, 'seq', axis=1, tiled=Tru...]
    unnamed x41 -> x16, local copies, waits for them, and re-layouts: 30.2 us -> 6.65 us
  transfers between devices with their start and end apart: 9 -> 0, of which waited for: 5 -> 0; matrix products, arithmetic and copies ran while one was open for 19% -> 0% of each run, Pallas kernels for 0% -> 0%
where the time goes in v1:
time: 180 us
  Pallas kernels  173 us (96%)
  local copies, waits for them, and re-layouts  6.65 us (4%)
    pallas_call x1, Pallas kernels, body(): pl.pallas_call(kernel, out_shape=(shape((128, 2240), BF), shape((128, 224...  173 us
    unnamed x16, local copies, waits for them, and re-layouts  6.65 us

profile of v1, /device:TPU:1, one launch (start us, length us, event | category | flops | bytes accessed | tf_op | source)
XLA Modules:
  0.0 180.2 jit_solution(1392654051057425321)
XLA Ops:
  0.6 172.9 %shard_map.109 = (bf16[128,2240]{1,0:T(8,128)(2,1)}, bf16[128,2240]{1,0:T(8,128)(2,1)}, bf16[128,1120]{1,0:T(8,128)(2,1)}, bf16[128,1120]{1,0:T(8,128)(2,1)}, f32[140,70]{1,0:T(8,128)}, /*index=5*/f32[70,140]{1,0:T(8,128)}) custom-call(bf16[128,2240]{1,0:T(8,128)(2,1)} %bitcast.10, bf16[128,1120]{1,0:T(8,128)(2,1)} %bitcast.12, bf16[128,1120]{1,0:T(8,128)(2,1)} %bitcast.13, ...), custom_call_target="tpu_custom_call" | custom-call | tf_op jit(solution)/shard_map/pallas_call | solution.py:571
  173.5 0.0 copy-start
  173.5 2.0 %copy.18 = bf16[2,64,2240]{2,1,0:T(8,128)(2,1)} copy(bf16[2,64,2240]{2,1,0:T(8,128)(2,1)} %bitcast.9) | data formatting | bytes 1146880
  175.5 0.0 copy-done
  175.5 0.0 copy-start.2
  175.5 0.8 copy.19
  176.3 0.3 copy-done.2
  176.6 0.0 copy-start.1
  176.6 0.7 copy.20
  177.3 0.4 copy-done.1
  177.7 0.0 copy-start.4
  177.7 0.7 copy.21
  178.4 0.2 copy-done.4
  178.6 0.0 copy-start.3
  178.6 0.6 copy.22
  179.2 0.3 copy-done.3
  179.5 0.6 copy.23
Async XLA Ops:
  173.5 2.0 %copy-start = (bf16[128,2240]{1,0:T(8,128)(2,1)S(1)}, bf16[128,2240]{1,0:T(8,128)(2,1)}, u32[]{:S(2)}) copy-start(bf16[128,2240]{1,0:T(8,128)(2,1)} %get-tuple-element.13) | copy-start | bytes 1720324
  175.5 1.1 copy-start.2
  176.6 1.1 copy-start.1
  177.7 0.9 copy-start.4
  178.6 0.9 copy-start.3

commit v2 on v1

--- a/solution.py
+++ b/solution.py
@@ -10,7 +10,7 @@
 MESH = pl.DeviceIdType.MESH
 VM = pltpu.VMEM
 SIZE = {"x": 4, "y": 4, "z": 8}
-ORDERS = (("x", "y", "z"), ("y", "z", "x"), ("z", "x", "y"))
+SCATTER = (("z", "x", "y"), ("x", "y", "z"), ("y", "x", "z"))
 PAIRS = ((0, 1), (1, 0), (1, 1), (2, 0), (2, 1), (3, 0), (3, 1))
 N_SEMS = 320
 
@@ -23,7 +23,8 @@
         self.y = lax.div(seq, 4)
         self.xl = lax.rem(lax.div(seq, 2), 2)
         self.c = lax.rem(seq, 2)
-        self.x = lax.div(dp, 8) * 2 + self.xl
+        self.xh = lax.div(dp, 8)
+        self.x = self.xh * 2 + self.xl
         self.p = self.y * 2 + self.xl
 
     def step(self, d, k):
@@ -84,43 +85,63 @@
             cp.wait_send()
 
 
-def gather(wire, me, buf, o):
-    open_ = []
+def gather(wire, me, buf, o, tile=None):
     sib = []
 
-    def piece(d, b, half=None):
-        return buf.at[(me.c,) + me.index(o, open_, d, b, half)]
-
-    def share(d, b, half=None):
-        ref = piece(d, b, half)
+    def share(ref):
         sib.append(wire.send(ref, ref, me.sibling()))
 
-    for n, d in enumerate(ORDERS[o]):
-        last = n == 2
-        if last:
-            share(d, getattr(me, d))
-        if d != "z":
-            own = piece(d, getattr(me, d))
-            cps = [wire.send(own, own, me.peer(d, k)) for k in range(1, SIZE[d])]
+    def piece(xh=None, z=None, y=None, xl=None, half=None):
+        every = slice(None)
+        i = (me.c,) + tuple(every if v is None else v for v in (xh, z, y, xl)) + (o,)
+        return buf.at[i if half is None else i + (half,)]
+
+    def direct(d, ref):
+        cps = [wire.send(ref, ref, me.peer(d, k)) for k in range(1, SIZE[d])]
+        yield
+        for cp in cps:
+            cp.wait_recv()
+
+    def ring(d, block):
+        share(block(getattr(me, d)))
+        steps = SIZE[d] // 2
+        for s in range(1, steps + 1):
+            hp, hm = (0, 1) if s == steps else (None, None)
+            fp = block(me.step(d, -(s - 1)), hp)
+            fm = block(me.step(d, s - 1), hm)
+            plus = wire.send(fp, fp, me.peer(d, 1))
+            minus = wire.send(fm, fm, me.peer(d, -1))
             yield
-            for k, cp in enumerate(cps, 1):
+            plus.wait_recv()
+            minus.wait_recv()
+            share(block(me.step(d, -s), hp))
+            share(block(me.step(d, s), hm))
+
+    if o == 0:
+        ref = piece(xh=me.xh, z=me.z, half=tile)
+        cp = wire.send(ref, ref, me.dev(x=3 - me.x))
+        yield
+        cp.wait_recv()
+        share(piece(z=me.z, half=tile))
+        for s in range(1, 5):
+            cps = []
+            for sign in (1, -1) if s < 4 else ((1, -1)[tile],):
+                ref = piece(z=me.step("z", -sign * (s - 1)), half=tile)
+                cps.append((sign, wire.send(ref, ref, me.peer("z", sign))))
+            yield
+            for sign, cp in cps:
                 cp.wait_recv()
-                if last:
-                    share(d, me.step(d, -k))
-        else:
-            for s in range(1, 5):
-                hp, hm = (0, 1) if s == 4 else (None, None)
-                fp = piece(d, me.step(d, -(s - 1)), hp)
-                fm = piece(d, me.step(d, s - 1), hm)
-                plus = wire.send(fp, fp, me.peer(d, 1))
-                minus = wire.send(fm, fm, me.peer(d, -1))
-                yield
-                plus.wait_recv()
-                minus.wait_recv()
-                if last:
-                    share(d, me.step(d, -s), hp)
-                    share(d, me.step(d, s), hm)
-        open_.append(d)
+                share(piece(z=me.step("z", -sign * s), half=tile))
+    elif o == 1:
+        yield from direct("z", piece(me.xh, me.z, me.y, me.xl))
+        yield from direct("y", piece(xh=me.xh, y=me.y, xl=me.xl))
+        yield from ring(
+            "x", lambda b, h=None: piece(xh=lax.div(b, 2), xl=lax.rem(b, 2), half=h)
+        )
+    else:
+        yield from direct("z", piece(me.xh, me.z, me.y, me.xl))
+        yield from direct("x", piece(xh=me.xh, y=me.y, xl=me.xl))
+        yield from ring("y", lambda b, h=None: piece(y=b, half=h))
     yield
     for cp in sib:
         cp.wait_recv()
@@ -128,7 +149,7 @@
 
 def scatter(wire, me, buf, o, rx, fin):
     rx = iter(rx)
-    dims = ORDERS[o]
+    dims = SCATTER[o]
     for n, d in enumerate(dims):
         open_ = dims[n + 1 :]
         last = n == 2
@@ -137,16 +158,17 @@
             return me.index(o, open_, d, me.step(d, k), half)
 
         own = at(0)
-        if d != "z":
-            slots = [next(rx) for _ in range(3)]
+        if d != "z" or n:
+            slots = [next(rx) for _ in range(1, SIZE[d])]
             cps = [
-                wire.send(buf.at[at(k)], slots[k - 1], me.peer(d, k)) for k in (1, 2, 3)
+                wire.send(buf.at[at(k)], slots[k - 1], me.peer(d, k))
+                for k in range(1, SIZE[d])
             ]
             yield
             acc = buf[own].astype(F32)
-            for k in range(3):
-                cps[k].wait_recv()
-                acc = acc + slots[k][...].astype(F32)
+            for cp, slot in zip(cps, slots):
+                cp.wait_recv()
+                acc = acc + slot[...].astype(F32)
         else:
             up = [next(rx) for _ in range(4)]
             down = [next(rx) for _ in range(4)]
@@ -172,7 +194,7 @@
 
 
 def scatter_slots(o):
-    dims = ORDERS[o]
+    dims = SCATTER[o]
     out = []
     for n, d in enumerate(dims):
         open_ = dims[n + 1 :]
@@ -186,8 +208,8 @@
         if "x" in open_:
             shape += (2,)
         tile = (16, 128)
-        if d != "z":
-            out += [VM(shape + (2,) + tile, BF)] * 3
+        if d != "z" or n:
+            out += [VM(shape + (2,) + tile, BF)] * (SIZE[d] - 1)
         else:
             out += ([VM(shape + tile, BF)] + [VM(shape + (2,) + tile, BF)] * 3) * 2
     return out
@@ -277,66 +299,69 @@
         cut.append(cut[-1] + n)
     slot_sets = [slots[cut[i] : cut[i + 1]] for i in range(6)]
 
+    wv_t = wv.reshape(2, 16, 48, 16, 128)
+    wo_t = wo.reshape(2, 16, 48, 16, 128)
+    shard = me.xh * 8 + me.z
     wvp[...] = jnp.zeros_like(wvp)
     wvp[0:140, 0:1120] = wv_in[...]
+    for l in range(5):
+        slab = wvp[:, pl.ds(pl.multiple_of((5 * me.c + l) * 128, 128), 128)]
+        wv_t[me.c, shard, 9 * l : 9 * l + 9] = slab.reshape(9, 16, 128)
+    wv_t[me.c, shard, 45:48] = jnp.zeros((3, 16, 128), BF)
     wop[...] = jnp.zeros_like(wop)
     wop[0:70, 0:2240] = wo_in[...]
-    xh = lax.div(me.x, 2)
-    for k in range(6):
-        t = 6 * me.p + k
-        r, l = lax.rem(t, 9), lax.div(t, 9)
-        wv[me.c, xh, me.z, me.y, me.xl, k // 2, k % 2] = wvp[
-            pl.ds(pl.multiple_of(r * 16, 16), 16),
-            pl.ds(pl.multiple_of((5 * me.c + l) * 128, 128), 128),
-        ]
-        r, l = lax.rem(t, 5), lax.div(t, 5)
-        wo[me.c, xh, me.z, me.y, me.xl, k // 2, k % 2] = wop[
-            pl.ds(pl.multiple_of(r * 16, 16), 16),
-            pl.ds(pl.multiple_of((9 * me.c + l) * 128, 128), 128),
-        ]
+    for l in range(9):
+        slab = wop[:, pl.ds(pl.multiple_of((9 * me.c + l) * 128, 128), 128)]
+        wo_t[me.c, shard, 5 * l : 5 * l + 5] = slab.reshape(5, 16, 128)
+    wo_t[me.c, shard, 45:48] = jnp.zeros((3, 16, 128), BF)
 
     peers = [me.peer("x", k) for k in (1, 2, 3)] + [me.peer("y", k) for k in (1, 2, 3)]
-    peers += [me.peer("z", 1), me.peer("z", -1), me.sibling()]
+    peers += [me.peer("z", k) for k in range(1, 8)] + [me.sibling()]
     peers += [me.row_peer(dy, 1) for dy in (1, 2, 3)]
     barrier = pltpu.get_barrier_semaphore()
     for dev in peers:
         pl.semaphore_signal(barrier, inc=1, device_id=dev, device_id_type=MESH)
     pl.semaphore_wait(barrier, len(peers))
 
-    ga = [gather(wire, me, wv, o) for o in range(3)]
-    gb = [gather(wire, me, wo, o) for o in range(3)]
-    step(ga)
+    a0 = [gather(wire, me, wv, 0, t) for t in range(2)]
+    b0 = [gather(wire, me, wo, 0, t) for t in range(2)]
+    a1, a2, b1, b2 = [[gather(wire, me, w, o)] for w in (wv, wo) for o in (1, 2)]
+
+    def go(*order):
+        for g in order:
+            step(g)
+
+    go(a1, a2, a0)
+    go(b1, b2, a0)
 
     tokp[...] = jnp.zeros_like(tokp)
     for i in range(16):
         tokp[:, 144 * i : 144 * i + 140] = tok[:, 140 * i : 140 * i + 140]
-    step(ga)
+    go(a1, a2, b1, b2, a0)
     qp[...] = jnp.zeros_like(qp)
     qp[:, 0:1120] = q_in[...]
     kp[...] = jnp.zeros_like(kp)
     kp[:, 0:1120] = k_in[...]
-    step(ga)
-    step(gb)
+    part1[...] = jnp.zeros_like(part1)
+    part2[...] = jnp.zeros_like(part2)
+    go(a1, a2, a0, b0)
+    att_p[...] = jnp.zeros_like(att_p)
+    gvp[me.c] = jnp.zeros((128, 1280), BF)
     cotp[me.c] = jnp.zeros((128, 2304), BF)
     cotp[me.c, :, 0:2240] = cot[...]
-    ex_cot = wire.send(cotp.at[me.c], cotp.at[me.c], me.sibling())
+    go(a0)
     for i in range(9):
         tok_t[me.c, 256 * i : 256 * i + 256] = tokp[:, 256 * i : 256 * i + 256].T
-    ex_tok = wire.send(tok_t.at[me.c], tok_t.at[me.c], me.sibling())
-    part1[...] = jnp.zeros_like(part1)
-    part2[...] = jnp.zeros_like(part2)
-    att_p[...] = jnp.zeros_like(att_p)
-    gvp[me.c] = jnp.zeros((128, 1280), BF)
     rsv_t = rs_v.reshape(16, 48, 16, 128)
     rso_t = rs_o.reshape(16, 48, 16, 128)
     rsv_t[:, 45:48] = jnp.zeros((16, 3, 16, 128), BF)
     rso_t[:, 45:48] = jnp.zeros((16, 3, 16, 128), BF)
-    while ga:
-        step(ga)
-        step(gb)
-
-    wv_t = wv.reshape(2, 16, 48, 16, 128)
-    wo_t = wo.reshape(2, 16, 48, 16, 128)
+    ghp[...] = jnp.zeros_like(ghp)
+    go(a1, a2, a0, b0, b1, b2, a1, a2)
+    go(a0, a1, a2)
+    ex_cot = wire.send(cotp.at[me.c], cotp.at[me.c], me.sibling())
+    ex_tok = wire.send(tok_t.at[me.c], tok_t.at[me.c], me.sibling())
+
     row = lax.broadcasted_iota(jnp.int32, (128, 128), 0) // 32
     col = lax.broadcasted_iota(jnp.int32, (128, 128), 1) // 32
     heads = (row == col).astype(F32)
@@ -355,6 +380,8 @@
             part = dot(tokp[:, 1152 * h : 1152 * h + 1152], slab)
             acc = part if acc is None else acc + part
         val[:, 128 * group[0] : 128 * (group[-1] + 1)] = acc.astype(BF)
+        if group[0] == 2:
+            step(b0)
 
     def lanes_of(g):
         return pl.ds(pl.multiple_of(g * 128, 128), 128)
@@ -378,12 +405,10 @@
             put(part1, img, g, t_dot(kf, val[rows, ln]), line)
             return carry
 
-        lax.fori_loop(0, 9, state, 0)
+        lax.fori_loop(0, 9, state, 0, unroll=3)
 
     s1 = [seq_sum(wire, me, part1, sib1, row1, tot1)]
-    while s1:
-        step(s1)
-        step(gb)
+    go(s1, b0, s1, s1, b1, b2, b0, s1, s1)
 
     for img in range(2):
         rows = slice(64 * img, 64 * img + 64)
@@ -402,15 +427,34 @@
             att_h[rows, ln] = ratio.astype(BF)
             return carry
 
-        lax.fori_loop(0, 9, attend, 0)
+        lax.fori_loop(0, 9, attend, 0, unroll=3)
     for i in range(16):
         att_p[:, 80 * i : 80 * i + 70] = att_h[:, 70 * i : 70 * i + 70]
     for i in range(5):
         att_t[me.c, 256 * i : 256 * i + 256] = att_p[:, 256 * i : 256 * i + 256].T
     ex_att = wire.send(att_t.at[me.c], att_t.at[me.c], me.sibling())
-
-    while gb:
-        step(gb)
+    while b0 or b1 or b2:
+        step(b1)
+        step(b2)
+        step(b0)
+
+    ex_cot.wait_recv()
+    ex_att.wait_recv()
+
+    cot_half = pl.ds(pl.multiple_of(me.c * 1152, 128), 1152)
+
+    def out_term(i, carry):
+        a = jnp.concatenate([att_t[s, pl.ds(pl.multiple_of(160 * i, 32), 160)] for s in (0, 1)], axis=1)
+        b = jnp.concatenate([cotp[0, :, cot_half], cotp[1, :, cot_half]], axis=0)
+        m = dot(a, b).astype(BF)
+        for l in range(9):
+            rso_t[pl.ds(2 * i, 2), 5 * l : 5 * l + 5] = m[:, 128 * l : 128 * l + 128].reshape(2, 5, 16, 128)
+        return carry
+
+    lax.fori_loop(0, 8, out_term, 0)
+    so = [scatter(wire, me, rs_o, o, slot_sets[o], fin_o) for o in range(3)]
+    so_ring = so[:1]
+    step(so)
 
     def out_rows(i, n):
         return jnp.concatenate(
@@ -421,12 +465,13 @@
             axis=1,
         )
 
-    ghp[...] = jnp.zeros_like(ghp)
     for i in range(4):
         gh = dot_t(cotp[me.c], out_rows(4 * i, 4))
         for j in range(4):
             at = 70 * (4 * i + j)
             ghp[:, at : at + 70] = gh[:, 80 * j : 80 * j + 70]
+        if i == 2:
+            step(so_ring)
 
     for img in range(2):
         rows = slice(64 * img, 64 * img + 64)
@@ -447,29 +492,16 @@
             put(part2, img, g, t_dot(qf, hi) + t_dot(qf, lo), line)
             return carry
 
-        lax.fori_loop(0, 9, grads, 0)
+        lax.fori_loop(0, 9, grads, 0, unroll=3)
 
     s2 = [seq_sum(wire, me, part2, sib2, row2, tot2)]
     step(s2)
     gq_o[...] = gqp[:, 0:1120]
-    ex_cot.wait_recv()
-    ex_att.wait_recv()
+    step(so_ring)
     step(s2)
 
-    cot_half = pl.ds(pl.multiple_of(me.c * 1152, 128), 1152)
-
-    def out_term(i, carry):
-        a = jnp.concatenate([att_t[s, pl.ds(pl.multiple_of(160 * i, 32), 160)] for s in (0, 1)], axis=1)
-        b = jnp.concatenate([cotp[0, :, cot_half], cotp[1, :, cot_half]], axis=0)
-        m = dot(a, b).astype(BF)
-        for l in range(9):
-            rso_t[pl.ds(2 * i, 2), 5 * l : 5 * l + 5] = m[:, 128 * l : 128 * l + 128].reshape(2, 5, 16, 128)
-        return carry
-
-    lax.fori_loop(0, 8, out_term, 0)
+    step(so_ring)
     step(s2)
-    so = [scatter(wire, me, rs_o, o, slot_sets[o], fin_o) for o in range(3)]
-    step(so)
     for i in range(9):
         slab = jnp.concatenate(
             [
@@ -480,6 +512,7 @@
         )
         width = min(256, 2240 - 256 * i)
         out_o[:, 256 * i : 256 * i + width] = dot(att_p[...], slab).astype(BF)[:, 0:width]
+    step(so)
     while s2:
         step(s2)
 
@@ -498,7 +531,7 @@
             gkp[rows, ln] = jnp.where(k > 0, part, 0.0).astype(BF)
             return carry
 
-        lax.fori_loop(0, 9, last_grads, 0)
+        lax.fori_loop(0, 9, last_grads, 0, unroll=3)
     ex_gv = wire.send(gvp.at[me.c], gvp.at[me.c], me.sibling())
     step(so)
     gk_o[...] = gkp[:, 0:1120]
@@ -517,8 +550,12 @@
 
     lax.fori_loop(0, 8, value_term, 0)
     sv = [scatter(wire, me, rs_v, o, slot_sets[3 + o], fin_v) for o in range(3)]
+    sv_ring = sv[:1]
     step(sv)
-    step(so)
+    while so:
+        step(so)
+    eo = [spread(wire, me, fin_o)]
+    step(eo)
 
     for i in range(4):
         w = jnp.concatenate(
@@ -532,14 +569,12 @@
         for j in range(4):
             at = 140 * (4 * i + j)
             gtok_o[:, at : at + 140] = gt[:, 144 * j : 144 * j + 140]
-        step(so)
+        if i < 3:
+            step(sv_ring)
+    step(eo)
     while sv:
-        step(so)
         step(sv)
-    while so:
-        step(so)
-
-    ends = [spread(wire, me, fin_o), spread(wire, me, fin_v)]
+    ends = [spread(wire, me, fin_v)] + eo
     while ends:
         step(ends)
     seq = me.p * 2 + me.c
@@ -559,6 +594,11 @@
     m = jnp.concatenate([slab_of(fin_ot, jnp.minimum(first + j, 17), 9, 5) for j in range(3)], axis=1)
     gwo_o[...] = pltpu.roll(m, lax.rem(384 - shift, 384), 1)[0:70, 0:140]
     wire.drain()
+
+
+def hand_over(*refs):
+    for i in range(6):
+        refs[6 + i][...] = refs[i][...]
 
 
 def body(tokens, q_raw, k_raw, w_value, w_out, cotangent):
@@ -626,6 +666,12 @@
         w_out,
         cotangent.reshape(128, 2240),
     )
+    outs = pl.pallas_call(
+        hand_over,
+        out_shape=tuple(shape(o.shape, o.dtype) for o in outs),
+        in_specs=[pl.BlockSpec(memory_space=VM)] * 6,
+        out_specs=(pl.BlockSpec(memory_space=VM),) * 6,
+    )(*outs)
     return (
         outs[0].reshape(2, 64, 2240),
         outs[1].reshape(2, 64, 2240),

time: 180 us -> 138 us (0.77)
  Pallas kernels: 173 us -> 137 us
  local copies, waits for them, and re-layouts: 6.65 us -> 0 us
    pallas_call x1, Pallas kernels: 173 us -> 134 us  [body(): pl.pallas_call(kernel, out_shape=(shape((128, 2240), BF), shape((128, 224...]
    unnamed x16 -> x0, local copies, waits for them, and re-layouts: 6.65 us -> none
    pallas_call x0 -> x1, Pallas kernels: none -> 2.72 us  [body(): pl.pallas_call(hand_over, out_shape=tuple((shape(o.shape, o.dtype) for o...]
where the time goes in v2:
time: 138 us
  Pallas kernels  137 us (99%)
    pallas_call x1, Pallas kernels, body(): pl.pallas_call(kernel, out_shape=(shape((128, 2240), BF), shape((128, 224...  134 us

profile of v2, /device:TPU:1, one launch (start us, length us, event | category | flops | bytes accessed | tf_op | source)
XLA Modules:
  0.0 137.8 jit_solution(17455926999176723894)
XLA Ops:
  0.6 134.4 %shard_map.109 = (bf16[128,2240]{1,0:T(8,128)(2,1)}, bf16[128,2240]{1,0:T(8,128)(2,1)}, bf16[128,1120]{1,0:T(8,128)(2,1)}, bf16[128,1120]{1,0:T(8,128)(2,1)}, f32[140,70]{1,0:T(8,128)}, /*index=5*/f32[70,140]{1,0:T(8,128)}) custom-call(bf16[128,2240]{1,0:T(8,128)(2,1)} %bitcast.8, bf16[128,1120]{1,0:T(8,128)(2,1)} %bitcast.10, bf16[128,1120]{1,0:T(8,128)(2,1)} %bitcast.11, ...), custom_call_target="tpu_custom_call" | custom-call | tf_op jit(solution)/shard_map/pallas_call | solution.py:611
  135.1 2.7 %shard_map.110 = (bf16[128,2240]{1,0:T(8,128)(2,1)}, bf16[128,2240]{1,0:T(8,128)(2,1)}, bf16[128,1120]{1,0:T(8,128)(2,1)}, bf16[128,1120]{1,0:T(8,128)(2,1)}, f32[140,70]{1,0:T(8,128)}, /*index=5*/f32[70,140]{1,0:T(8,128)}) custom-call(bf16[128,2240]{1,0:T(8,128)(2,1)} %get-tuple-element.18.refs_0_, bf16[128,2240]{1,0:T(8,128)(2,1)} %get-tuple-element.19.refs_1_, ...), custom_call_target="tpu_custom_call" | custom-call | tf_op jit(solution)/shard_map/pallas_call | solution.py:669

commit v3 on v2

--- a/solution.py
+++ b/solution.py
@@ -43,9 +43,9 @@
     def sibling(self):
         return self.dev(c=1 - self.c)
 
-    def row_peer(self, dy, dx):
+    def row_peer(self, dy, dx, c=None):
         xl = lax.rem(self.xl + dx, 2)
-        return self.dev(y=self.step("y", dy), x=self.x - self.xl + xl)
+        return self.dev(y=self.step("y", dy), x=self.x - self.xl + xl, c=c)
 
     def index(self, o, open_, d, b, half=None):
         co = {"x": self.x, "y": self.y, "z": self.z}
@@ -227,6 +227,51 @@
     cp.wait_recv()
 
 
+def span(c, p, div):
+    first = 5 * c + div(2 * p, 3)
+    final = 5 * c + div(6 * p + 5, 9)
+    return div(128 * first, 70), div(128 * final + 127, 70)
+
+
+def deliver(wire, me, fin):
+    base = N_SEMS - 16
+    seq = me.p * 2 + me.c
+    mine = fin.at[me.c, me.p]
+    first, final = span(me.c, me.p, lax.div)
+    ends = []
+    for e in range(5):
+        to = first + e
+        cp = pltpu.make_async_remote_copy(
+            src_ref=mine,
+            dst_ref=mine,
+            send_sem=wire.sems.at[0, base + e],
+            recv_sem=wire.sems.at[1, base + me.c * 8 + me.p],
+            device_id=(me.xh * 8 + me.z, jnp.minimum(to, 15)),
+            device_id_type=MESH,
+        )
+        used = (to <= final) & (to <= 15) & (to != seq)
+        pl.when(used)(cp.start)
+        ends.append((used, cp))
+    yield
+    for c in range(2):
+        for p in range(8):
+            lo, hi = span(c, p, lambda a, b: a // b)
+            if lo > 15:
+                continue
+            used = (seq >= lo) & (seq <= hi) & (seq != 2 * p + c)
+            cp = pltpu.make_async_remote_copy(
+                src_ref=fin.at[c, p],
+                dst_ref=fin.at[c, p],
+                send_sem=wire.sems.at[0, base + 5],
+                recv_sem=wire.sems.at[1, base + c * 8 + p],
+                device_id=me.sibling(),
+                device_id_type=MESH,
+            )
+            pl.when(used)(cp.wait_recv)
+    for used, cp in ends:
+        pl.when(used)(cp.wait_send)
+
+
 def seq_sum(wire, me, part, from_sib, from_row, total):
     cp = wire.send(part.at[1 - me.c], from_sib, me.sibling())
     yield
@@ -285,12 +330,25 @@
 
 
 def kernel(
-    tok, q_in, k_in, wv_in, wo_in, cot,
-    out_o, gtok_o, gq_o, gk_o, gwv_o, gwo_o,
-    sems, wv, wo, wvp, wop, tokp, tok_t, cotp, qp, kp, val, attf, denf, att_h, att_p, att_t,
+    tok_h, q_h, k_h, wv_in, wo_in, cot_h,
+    out_h, gtok_h, gq_h, gk_h, gwv_o, gwo_o,
+    local, tok, q_in, k_in, cot, out_o, gtok_o, gq_o, gk_o, sems, wv, wo, wvp, wop, tokp, tok_t, cotp, qp, kp, val, attf, denf, att_h, att_p, att_t,
     ghp, gvp, gqp, gkp, part1, part2, sib1, sib2, row1, row2, tot1, tot2,
     rs_v, rs_o, fin_v, fin_o, *slots,
 ):
+    ins = [
+        pltpu.make_async_copy(a, b, local.at[i])
+        for i, (a, b) in enumerate(((tok_h, tok), (q_h, q_in), (k_h, k_in), (cot_h, cot)))
+    ]
+    for cp in ins:
+        cp.start()
+    leaving = []
+
+    def leave(src, dst):
+        cp = pltpu.make_async_copy(src, dst, local.at[4 + len(leaving)])
+        cp.start()
+        leaving.append(cp)
+
     me = Place()
     wire = Wire(sems)
     per = [len(scatter_slots(o)) for o in range(3)]
@@ -318,6 +376,7 @@
     peers = [me.peer("x", k) for k in (1, 2, 3)] + [me.peer("y", k) for k in (1, 2, 3)]
     peers += [me.peer("z", k) for k in range(1, 8)] + [me.sibling()]
     peers += [me.row_peer(dy, 1) for dy in (1, 2, 3)]
+    peers += [me.row_peer(dy, dx, 1 - me.c) for dy, dx in PAIRS]
     barrier = pltpu.get_barrier_semaphore()
     for dev in peers:
         pl.semaphore_signal(barrier, inc=1, device_id=dev, device_id_type=MESH)
@@ -334,6 +393,8 @@
     go(a1, a2, a0)
     go(b1, b2, a0)
 
+    for cp in ins:
+        cp.wait()
     tokp[...] = jnp.zeros_like(tokp)
     for i in range(16):
         tokp[:, 144 * i : 144 * i + 140] = tok[:, 140 * i : 140 * i + 140]
@@ -497,6 +558,7 @@
     s2 = [seq_sum(wire, me, part2, sib2, row2, tot2)]
     step(s2)
     gq_o[...] = gqp[:, 0:1120]
+    leave(gq_o, gq_h)
     step(so_ring)
     step(s2)
 
@@ -535,6 +597,8 @@
     ex_gv = wire.send(gvp.at[me.c], gvp.at[me.c], me.sibling())
     step(so)
     gk_o[...] = gkp[:, 0:1120]
+    leave(gk_o, gk_h)
+    leave(out_o, out_h)
     ex_tok.wait_recv()
     ex_gv.wait_recv()
 
@@ -571,10 +635,12 @@
             gtok_o[:, at : at + 140] = gt[:, 144 * j : 144 * j + 140]
         if i < 3:
             step(sv_ring)
+    step(sv)
     step(eo)
     while sv:
         step(sv)
-    ends = [spread(wire, me, fin_v)] + eo
+    leave(gtok_o, gtok_h)
+    ends = [deliver(wire, me, fin_v)] + eo
     while ends:
         step(ends)
     seq = me.p * 2 + me.c
@@ -594,6 +660,8 @@
     m = jnp.concatenate([slab_of(fin_ot, jnp.minimum(first + j, 17), 9, 5) for j in range(3)], axis=1)
     gwo_o[...] = pltpu.roll(m, lax.rem(384 - shift, 384), 1)[0:70, 0:140]
     wire.drain()
+    for cp in leaving:
+        cp.wait()
 
 
 def hand_over(*refs):
@@ -618,9 +686,20 @@
             shape((140, 70), F32),
             shape((70, 140), F32),
         ),
-        in_specs=[pl.BlockSpec(memory_space=VM)] * 6,
-        out_specs=(pl.BlockSpec(memory_space=VM),) * 6,
+        in_specs=[pl.BlockSpec(memory_space=m) for m in (pl.ANY, pl.ANY, pl.ANY, VM, VM, pl.ANY)],
+        out_specs=tuple(
+            pl.BlockSpec(memory_space=m) for m in (pl.ANY, pl.ANY, pl.ANY, pl.ANY, VM, VM)
+        ),
         scratch_shapes=[
+            pltpu.SemaphoreType.DMA((8,)),
+            VM((128, 2240), BF),
+            VM((128, 1120), BF),
+            VM((128, 1120), BF),
+            VM((128, 2240), BF),
+            VM((128, 2240), BF),
+            VM((128, 2240), BF),
+            VM((128, 1120), BF),
+            VM((128, 1120), BF),
             pltpu.SemaphoreType.DMA((2, N_SEMS)),
             weight,
             weight,

time: 138 us -> 132 us (0.957)
  Pallas kernels: 137 us -> 131 us
    pallas_call x1, Pallas kernels: 134 us -> 129 us  [body(): pl.pallas_call(kernel, out_shape=(shape((128, 2240), BF), shape((128, 224...]
where the time goes in v3:
time: 132 us
  Pallas kernels  131 us (99%)
    pallas_call x1, Pallas kernels, body(): pl.pallas_call(kernel, out_shape=(shape((128, 2240), BF), shape((128, 224...  129 us
    pallas_call x1, Pallas kernels, body(): pl.pallas_call(hand_over, out_shape=tuple((shape(o.shape, o.dtype) for o...  2.72 us

profile of v3, /device:TPU:1, one launch (start us, length us, event | category | flops | bytes accessed | tf_op | source)
XLA Modules:
  0.0 132.0 jit_solution(14892198169143198409)
XLA Ops:
  0.6 128.6 %shard_map.109 = (bf16[128,2240]{1,0:T(8,128)(2,1)}, bf16[128,2240]{1,0:T(8,128)(2,1)}, bf16[128,1120]{1,0:T(8,128)(2,1)}, bf16[128,1120]{1,0:T(8,128)(2,1)}, f32[140,70]{1,0:T(8,128)}, /*index=5*/f32[70,140]{1,0:T(8,128)}) custom-call(bf16[128,2240]{1,0:T(8,128)(2,1)} %bitcast.8, bf16[128,1120]{1,0:T(8,128)(2,1)} %bitcast.10, bf16[128,1120]{1,0:T(8,128)(2,1)} %bitcast.11, ...), custom_call_target="tpu_custom_call" | custom-call | tf_op jit(solution)/shard_map/pallas_call | solution.py:679
  129.3 2.7 %shard_map.110 = (bf16[128,2240]{1,0:T(8,128)(2,1)}, bf16[128,2240]{1,0:T(8,128)(2,1)}, bf16[128,1120]{1,0:T(8,128)(2,1)}, bf16[128,1120]{1,0:T(8,128)(2,1)}, f32[140,70]{1,0:T(8,128)}, /*index=5*/f32[70,140]{1,0:T(8,128)}) custom-call(bf16[128,2240]{1,0:T(8,128)(2,1)} %get-tuple-element.18.refs_0_, bf16[128,2240]{1,0:T(8,128)(2,1)} %get-tuple-element.19.refs_1_, ...), custom_call_target="tpu_custom_call" | custom-call | tf_op jit(solution)/shard_map/pallas_call | solution.py:748

commit v4 on v3

--- a/solution.py
+++ b/solution.py
@@ -614,8 +614,8 @@
 
     lax.fori_loop(0, 8, value_term, 0)
     sv = [scatter(wire, me, rs_v, o, slot_sets[3 + o], fin_v) for o in range(3)]
-    sv_ring = sv[:1]
-    step(sv)
+    sv_ring, sv_direct = sv[:1], sv[1:]
+    go(sv_direct, sv_ring)
     while so:
         step(so)
     eo = [spread(wire, me, fin_o)]
@@ -635,10 +635,9 @@
             gtok_o[:, at : at + 140] = gt[:, 144 * j : 144 * j + 140]
         if i < 3:
             step(sv_ring)
-    step(sv)
-    step(eo)
-    while sv:
-        step(sv)
+    go(sv_direct, sv_ring, eo)
+    while sv_direct or sv_ring:
+        go(sv_direct, sv_ring)
     leave(gtok_o, gtok_h)
     ends = [deliver(wire, me, fin_v)] + eo
     while ends:

time: 132 us -> 130 us (0.985)
  Pallas kernels: 131 us -> 129 us
    pallas_call x1, Pallas kernels: 129 us -> 126 us  [body(): pl.pallas_call(kernel, out_shape=(shape((128, 2240), BF), shape((128, 224...]
where the time goes in v4:
time: 130 us; the launch traced here: 129 us
  Pallas kernels  129 us (99%)
    pallas_call x1, Pallas kernels, body(): pl.pallas_call(kernel, out_shape=(shape((128, 2240), BF), shape((128, 224...  126 us
    pallas_call x1, Pallas kernels, body(): pl.pallas_call(hand_over, out_shape=tuple((shape(o.shape, o.dtype) for o...  2.72 us

profile of v4, /device:TPU:1, one launch (start us, length us, event | category | flops | bytes accessed | tf_op | source)
XLA Modules:
  0.0 129.5 jit_solution(12848540817394336530)
XLA Ops:
  0.6 126.1 %shard_map.109 = (bf16[128,2240]{1,0:T(8,128)(2,1)}, bf16[128,2240]{1,0:T(8,128)(2,1)}, bf16[128,1120]{1,0:T(8,128)(2,1)}, bf16[128,1120]{1,0:T(8,128)(2,1)}, f32[140,70]{1,0:T(8,128)}, /*index=5*/f32[70,140]{1,0:T(8,128)}) custom-call(bf16[128,2240]{1,0:T(8,128)(2,1)} %bitcast.8, bf16[128,1120]{1,0:T(8,128)(2,1)} %bitcast.10, bf16[128,1120]{1,0:T(8,128)(2,1)} %bitcast.11, ...), custom_call_target="tpu_custom_call" | custom-call | tf_op jit(solution)/shard_map/pallas_call | solution.py:678
  126.7 2.7 %shard_map.110 = (bf16[128,2240]{1,0:T(8,128)(2,1)}, bf16[128,2240]{1,0:T(8,128)(2,1)}, bf16[128,1120]{1,0:T(8,128)(2,1)}, bf16[128,1120]{1,0:T(8,128)(2,1)}, f32[140,70]{1,0:T(8,128)}, /*index=5*/f32[70,140]{1,0:T(8,128)}) custom-call(bf16[128,2240]{1,0:T(8,128)(2,1)} %get-tuple-element.18.refs_0_, bf16[128,2240]{1,0:T(8,128)(2,1)} %get-tuple-element.19.refs_1_, ...), custom_call_target="tpu_custom_call" | custom-call | tf_op jit(solution)/shard_map/pallas_call | solution.py:747

commit v5 on v4

--- a/solution.py
+++ b/solution.py
@@ -574,7 +574,8 @@
         )
         width = min(256, 2240 - 256 * i)
         out_o[:, 256 * i : 256 * i + width] = dot(att_p[...], slab).astype(BF)[:, 0:width]
-    step(so)
+    step(s2)
+    go(so[1:], so_ring)
     while s2:
         step(s2)
 
@@ -595,7 +596,7 @@
 
         lax.fori_loop(0, 9, last_grads, 0, unroll=3)
     ex_gv = wire.send(gvp.at[me.c], gvp.at[me.c], me.sibling())
-    step(so)
+    go(so[1:], so_ring)
     gk_o[...] = gkp[:, 0:1120]
     leave(gk_o, gk_h)
     leave(out_o, out_h)

time: 130 us -> 134 us (1.031)
  Pallas kernels: 129 us -> 133 us
    pallas_call x1, Pallas kernels: 126 us -> 130 us  [body(): pl.pallas_call(kernel, out_shape=(shape((128, 2240), BF), shape((128, 224...]
where the time goes in v5:
time: 134 us
  Pallas kernels  133 us (99%)
    pallas_call x1, Pallas kernels, body(): pl.pallas_call(kernel, out_shape=(shape((128, 2240), BF), shape((128, 224...  130 us
    pallas_call x1, Pallas kernels, body(): pl.pallas_call(hand_over, out_shape=tuple((shape(o.shape, o.dtype) for o...  2.72 us

profile of v5, /device:TPU:1, one launch (start us, length us, event | category | flops | bytes accessed | tf_op | source)
XLA Modules:
  0.0 133.8 jit_solution(6844194608831102460)
XLA Ops:
  0.6 130.4 %shard_map.109 = (bf16[128,2240]{1,0:T(8,128)(2,1)}, bf16[128,2240]{1,0:T(8,128)(2,1)}, bf16[128,1120]{1,0:T(8,128)(2,1)}, bf16[128,1120]{1,0:T(8,128)(2,1)}, f32[140,70]{1,0:T(8,128)}, /*index=5*/f32[70,140]{1,0:T(8,128)}) custom-call(bf16[128,2240]{1,0:T(8,128)(2,1)} %bitcast.8, bf16[128,1120]{1,0:T(8,128)(2,1)} %bitcast.10, bf16[128,1120]{1,0:T(8,128)(2,1)} %bitcast.11, ...), custom_call_target="tpu_custom_call" | custom-call | tf_op jit(solution)/shard_map/pallas_call | solution.py:679
  131.0 2.7 %shard_map.110 = (bf16[128,2240]{1,0:T(8,128)(2,1)}, bf16[128,2240]{1,0:T(8,128)(2,1)}, bf16[128,1120]{1,0:T(8,128)(2,1)}, bf16[128,1120]{1,0:T(8,128)(2,1)}, f32[140,70]{1,0:T(8,128)}, /*index=5*/f32[70,140]{1,0:T(8,128)}) custom-call(bf16[128,2240]{1,0:T(8,128)(2,1)} %get-tuple-element.18.refs_0_, bf16[128,2240]{1,0:T(8,128)(2,1)} %get-tuple-element.19.refs_1_, ...), custom_call_target="tpu_custom_call" | custom-call | tf_op jit(solution)/shard_map/pallas_call | solution.py:748
